TPU v7x, 512 devices: a whole 4x4x16 slice. The times are simulated.
512 devices in a mesh: aux: 64 (over y, z), occ: 8 (over x, core).
Axes of the slice: x: 4, y: 4, z: 16, core: 2. Of those that a mesh axis runs over, the one named last changes fastest.
Arguments:
- factor_tiles: bfloat16 [128, 24, 4, 128, 128], P('aux'), may hold values from -1 to 1
- tile_cols: int32 [128, 24, 4], P('aux'), may hold values from 0 to 23, as said below
- coeffs: bfloat16 [3072, 256], P(None, 'occ'), may hold values from -0.25 to 0.25
- pair_owner: int32 [576], P('aux'), may hold values from 0 to 575, each once
Outputs:
- exchange_tiles: float32 [576, 128, 128], P('aux', 'occ')
Inputs may be any that keep to these rules, and one draw needn't show every extreme that they name: `tile_cols`: for each auxiliary function and basis block row, the 4 listed column blocks are distinct. `pair_owner`: each basis block pair appears exactly once.
All inputs are finite; a program needn't handle non-finite values.
Results may differ from a plain program's by a relative error of at most 0.0015.
Values may be sent and summed in bfloat16 or wider, within the bound.
A program may use at most 128 MiB of HBM per device.

v0:
```python
import jax
import jax.numpy as jnp
from jax import lax
from jax.sharding import PartitionSpec as P


def shards(factor_tiles, tile_cols, coeffs, pair_owner):
    aux_count = factor_tiles.shape[0]
    block_count = factor_tiles.shape[1]
    tile_width = factor_tiles.shape[3]
    local_occ = coeffs.shape[1]
    blocks = coeffs.reshape(block_count, tile_width, local_occ)
    picked = blocks[tile_cols]
    halves = jnp.einsum(
        "qmsrl,qmsli->mrqi", factor_tiles, picked, preferred_element_type=jnp.float32
    ).astype(jnp.bfloat16)
    halves = halves.reshape(block_count, tile_width, aux_count * local_occ)
    row_blocks = pair_owner // block_count
    col_blocks = pair_owner % block_count
    gathered = lax.all_gather(halves, "aux", axis=2, tiled=True)
    row_part = jnp.take(gathered, row_blocks, axis=0)
    col_part = jnp.take(gathered, col_blocks, axis=0)
    partial_tiles = jnp.einsum(
        "sbw,scw->sbc", row_part, col_part, preferred_element_type=jnp.float32
    )
    summed = lax.psum(partial_tiles, "occ")
    share_rows = tile_width // lax.axis_size("occ")
    return lax.dynamic_slice_in_dim(summed, lax.axis_index("occ") * share_rows, share_rows, 1)


def solution(mesh):
    placed = (P("aux", None, None, None, None), P("aux", None, None), P(None, "occ"), P("aux"))
    return jax.shard_map(
        shards, mesh=mesh, in_specs=placed, out_specs=P("aux", "occ", None), check_vma=False
    )
```

profile of v0, /device:TPU:8, one launch (start us, length us, event | category | flops | bytes accessed | tf_op | source)
XLA Modules:
  0.0 413.8 jit_solution(6229224219525203429)
XLA Ops:
  6.5 0.0 copy-start
  6.5 0.0 all-gather.2.cloned.1.call-start
  6.5 0.9 copy-done
  7.5 0.7 compare_select_fusion
  8.2 0.1 copy.15
  8.3 0.1 reshape.31
  8.4 0.0 copy-start.2
  8.4 0.9 gather_fusion
  9.3 5.0 %fusion.14 = bf16[24,2,32,128]{3,2,1,0:T(8,128)(2,1)S(1)} fusion(bf16[2,24,4,128,128]{4,3,2,1,0:T(8,128)(2,1)} %param.6, bf16[2,24,4,128,32]{3,4,2,1,0:T(8,128)(2,1)S(1)} %bitcast.14), kind=kOutput, calls=%fused_computation.13 | convolution fusion | flops 201523200 | bytes 8257536 | tf_op jit(solution)/shard_map/qmsrl,qmsli->mrqi/dot_general | solution.py:14
  14.3 1.0 copy.19
  15.3 0.0 all-gather.2.cloned.1.call-update
  15.3 0.0 all-reduce.2.cloned.1.call-start
  15.4 0.0 copy-done.2
  15.4 247.6 %all-gather.2.cloned.1.call-done = bf16[24,128,4096]{1,0,2:T(8,128)(2,1)} async-done(((bf16[24,128,64]{1,0,2:T(8,128)(2,1)}), bf16[24,128,4096]{1,0,2:T(8,128)(2,1)}) %all-gather.2.cloned.1.call-update) | async-done | bytes 25165840 | tf_op jit(solution)/shard_map/all_gather | solution.py:20
  263.0 31.6 %copy.20 = bf16[24,128,4096]{2,1,0:T(8,128)(2,1)} copy(bf16[24,128,4096]{1,0,2:T(8,128)(2,1)} %all-gather.2.cloned.1.call-done) | data formatting | bytes 50331648 | tf_op jit(solution)/shard_map/all_gather | solution.py:20
  294.6 13.2 %gather_fusion.2 = bf16[9,128,4096]{2,1,0:T(8,128)(2,1)} fusion(bf16[24,128,4096]{2,1,0:T(8,128)(2,1)} %copy.20, s32[1024]{0:T(1024)S(1)} %get-tuple-element.12), kind=kCustom, calls=%fused_computation.1.clone | custom fusion | bytes 18874404 | tf_op jit(solution)/shard_map/jit(_take)/gather | solution.py:22
  307.8 13.3 %gather_fusion.1 = bf16[9,128,4096]{2,1,0:T(8,128)(2,1)} fusion(bf16[24,128,4096]{2,1,0:T(8,128)(2,1)} %copy.20, s32[1024]{0:T(1024)S(1)} %get-tuple-element.13), kind=kCustom, calls=%fused_computation.clone | custom fusion | bytes 18874404 | tf_op jit(solution)/shard_map/jit(_take)/gather | solution.py:21
  321.1 0.0 copy-start.1
  321.1 10.0 %fusion = f32[9,128,128]{2,1,0:T(8,128)} fusion(bf16[9,128,4096]{2,1,0:T(8,128)(2,1)} %gather_fusion.2, bf16[9,128,4096]{2,1,0:T(8,128)(2,1)} %gather_fusion.1, pred[9]{0:T(512)(128)(4,1)S(1)} %get-tuple-element.10, pred[9]{0:T(512)(128)(4,1)S(1)} %get-tuple-element.6), kind=kOutput, calls=%fused_computation.3 | convolution fusion | flops 1217396736 | bytes 19464210 | tf_op jit(solution)/shard_map/sbw,scw->sbc/dot_general | solution.py:23
  331.1 0.0 all-reduce.2.cloned.1.call-update
  331.1 74.3 %all-reduce.2.cloned.1.call-done = f32[9,128,128]{2,1,0:T(8,128)} async-done(((f32[9,128,128]{2,1,0:T(8,128)}), f32[9,128,128]{2,1,0:T(8,128)}) %all-reduce.2.cloned.1.call-update) | async-done | bytes 589840 | tf_op jit(solution)/shard_map/psum | solution.py:26
  405.4 1.5 constant_dynamic-slice_fusion
  406.9 0.0 copy-done.1
  (4 shorter events, 0.1 us)
Async XLA Ops:
  6.5 0.9 copy-start
  6.5 256.5 %all-gather.2.cloned.1.call-start = ((), (), s32[]{:S(2)}) async-start(), calls=%async_computation | async-start | bytes 25559040 | tf_op jit(solution)/shard_map/all_gather | solution.py:20
  8.4 7.0 %copy-start.2 = (s32[9]{0:T(128)S(1)}, s32[9]{0:T(128)}, u32[]{:S(2)}) copy-start(s32[9]{0:T(128)} %param.9) | copy-start | bytes 112
  15.3 390.1 %all-reduce.2.cloned.1.call-start = ((), (), s32[]{:S(2)}) async-start(), calls=%async_computation.1 | async-start | bytes 1179648 | tf_op jit(solution)/shard_map/psum | solution.py:26
  321.1 85.8 %copy-start.1 = (bf16[3072,32]{0,1:T(8,128)(2,1)S(1)}, bf16[3072,32]{0,1:T(8,128)(2,1)}, u32[]{:S(2)}) copy-start(bf16[3072,32]{0,1:T(8,128)(2,1)} %param.8) | copy-start | bytes 589828
Sparse Core Ops, SparseCore 0:
  15.4 247.5 all-gather.1
  331.3 74.0 all-reduce.1
where the time goes:
time: 415 us; the launch traced here: 414 us
  waiting for transfers between devices  322 us (78%)
  local copies, waits for them, and re-layouts  62.7 us (15%)
  matrix products  15 us (4%)
  between operations  13.5 us (3%)
    all_gather x1, waiting for transfers between devices, shards(): gathered = lax.all_gather(halves, 'aux', axis=2, tiled=True)  248 us
    psum x1, waiting for transfers between devices, shards(): summed = lax.psum(partial_tiles, 'occ')  74.3 us
    all_gather x1, local copies, waits for them, and re-layouts, shards(): gathered = lax.all_gather(halves, 'aux', axis=2, tiled=True)  31.6 us
    gather x1, local copies, waits for them, and re-layouts, shards(): row_part = jnp.take(gathered, row_blocks, axis=0)  13.3 us
    gather x1, local copies, waits for them, and re-layouts, shards(): col_part = jnp.take(gathered, col_blocks, axis=0)  13.2 us
    dot_general x1, matrix products, shards(): jnp.einsum('sbw,scw->sbc', row_part, col_part, preferred_element_type=jnp...  10 us
  transfers between devices with their start and end apart: 2, of which 2 were waited for; matrix products, arithmetic and copies ran while one was open for 0% of the time, Pallas kernels for 0%

commit v1 on v0

--- a/solution.py
+++ b/solution.py
@@ -23,7 +23,9 @@
     partial_tiles = jnp.einsum(
         "sbw,scw->sbc", row_part, col_part, preferred_element_type=jnp.float32
     )
-    summed = lax.psum(partial_tiles, "occ")
+    summed = partial_tiles
+    for hop in (1, 2, 4):
+        summed = summed + lax.ppermute(summed, "occ", [(dev, dev ^ hop) for dev in range(8)])
     share_rows = tile_width // lax.axis_size("occ")
     return lax.dynamic_slice_in_dim(summed, lax.axis_index("occ") * share_rows, share_rows, 1)
 

time: 415 us -> 379 us (0.913)
  the two profiles are of different devices: /device:TPU:8 before, /device:TPU:2 now
where the time goes in v1:
time: 379 us; the launch traced here: 378 us
  waiting for transfers between devices  280 us (74%)
  local copies, waits for them, and re-layouts  60.9 us (16%)
  matrix products  14.1 us (4%)
  between operations  13.5 us (4%)
  starting transfers between devices  8.38 us (2%)
    all_gather x1, waiting for transfers between devices, shards(): gathered = lax.all_gather(halves, 'aux', axis=2, tiled=True)  249 us
    all_gather x1, local copies, waits for them, and re-layouts, shards(): gathered = lax.all_gather(halves, 'aux', axis=2, tiled=True)  31.4 us
    ppermute x3, waiting for transfers between devices, shards(): lax.ppermute(summed, 'occ', [(dev, dev ^ hop) for dev in range(8)])  30.7 us
    gather x1, local copies, waits for them, and re-layouts, shards(): row_part = jnp.take(gathered, row_blocks, axis=0)  13.3 us
    gather x1, local copies, waits for them, and re-layouts, shards(): col_part = jnp.take(gathered, col_blocks, axis=0)  13.2 us
    dot_general x1, matrix products, shards(): jnp.einsum('sbw,scw->sbc', row_part, col_part, preferred_element_type=jnp...  9.19 us
    ppermute x3, starting transfers between devices, shards(): lax.ppermute(summed, 'occ', [(dev, dev ^ hop) for dev in range(8)])  8.38 us
  transfers between devices with their start and end apart: 4, of which 4 were waited for; matrix products, arithmetic and copies ran while one was open for 0% of the time, Pallas kernels for 0%

profile of v1, /device:TPU:2, one launch (start us, length us, event | category | flops | bytes accessed | tf_op | source)
XLA Modules:
  0.0 378.1 jit_solution(11418957022222466713)
XLA Ops:
  6.5 0.0 copy-start
  6.5 0.9 copy-done
  7.5 0.7 compare_select_fusion
  8.2 0.1 copy.15
  8.3 0.1 reshape.31
  8.4 0.0 copy-start.2
  8.4 0.9 gather_fusion
  9.3 5.0 %fusion.14 = bf16[24,2,32,128]{3,2,1,0:T(8,128)(2,1)S(1)} fusion(bf16[2,24,4,128,128]{4,3,2,1,0:T(8,128)(2,1)} %param.6, bf16[2,24,4,128,32]{3,4,2,1,0:T(8,128)(2,1)S(1)} %bitcast.14), kind=kOutput, calls=%fused_computation.13 | convolution fusion | flops 201523200 | bytes 8257536 | tf_op jit(solution)/shard_map/qmsrl,qmsli->mrqi/dot_general | solution.py:14
  14.3 1.0 copy.19
  15.3 0.0 all-gather.2.cloned.1.call-update
  15.4 249.0 %all-gather.2.cloned.1.call-done = bf16[24,128,4096]{1,0,2:T(8,128)(2,1)} async-done(((bf16[24,128,64]{1,0,2:T(8,128)(2,1)}), bf16[24,128,4096]{1,0,2:T(8,128)(2,1)}) %all-gather.2.cloned.1.call-update) | async-done | bytes 25165840 | tf_op jit(solution)/shard_map/all_gather | solution.py:20
  264.3 31.4 %copy.20 = bf16[24,128,4096]{2,1,0:T(8,128)(2,1)} copy(bf16[24,128,4096]{1,0,2:T(8,128)(2,1)} %all-gather.2.cloned.1.call-done) | data formatting | bytes 50331648 | tf_op jit(solution)/shard_map/all_gather | solution.py:20
  295.7 13.2 %gather_fusion.2 = bf16[9,128,4096]{2,1,0:T(8,128)(2,1)} fusion(bf16[24,128,4096]{2,1,0:T(8,128)(2,1)} %copy.20, s32[1024]{0:T(1024)S(1)} %get-tuple-element.12), kind=kCustom, calls=%fused_computation.1.clone | custom fusion | bytes 18874404 | tf_op jit(solution)/shard_map/jit(_take)/gather | solution.py:22
  308.9 13.3 %gather_fusion.1 = bf16[9,128,4096]{2,1,0:T(8,128)(2,1)} fusion(bf16[24,128,4096]{2,1,0:T(8,128)(2,1)} %copy.20, s32[1024]{0:T(1024)S(1)} %get-tuple-element.13), kind=kCustom, calls=%fused_computation.clone | custom fusion | bytes 18874404 | tf_op jit(solution)/shard_map/jit(_take)/gather | solution.py:21
  322.2 9.2 %fusion = f32[9,128,128]{2,1,0:T(8,128)S(1)} fusion(bf16[9,128,4096]{2,1,0:T(8,128)(2,1)} %gather_fusion.2, bf16[9,128,4096]{2,1,0:T(8,128)(2,1)} %gather_fusion.1, pred[9]{0:T(512)(128)(4,1)S(1)} %get-tuple-element.10, pred[9]{0:T(512)(128)(4,1)S(1)} %get-tuple-element.6), kind=kOutput, calls=%fused_computation.3 | convolution fusion | flops 1217396736 | bytes 19464210 | tf_op jit(solution)/shard_map/sbw,scw->sbc/dot_general | solution.py:23
  331.4 1.9 collective-permute-start
  333.3 2.0 collective-permute-done
  335.3 0.1 add.31
  335.3 2.5 collective-permute-start.1
  337.8 14.8 %collective-permute-done.1 = f32[9,128,128]{2,1,0:T(8,128)S(1)} collective-permute-done((f32[9,128,128]{2,1,0:T(8,128)S(1)}, f32[9,128,128]{2,1,0:T(8,128)S(1)}, u32[]{:S(2)}, u32[]{:S(2)}) %collective-permute-start.1) | collective-permute-done | bytes 589856 | tf_op jit(solution)/shard_map/ppermute | solution.py:28
  352.6 0.1 add.32
  352.7 4.0 %collective-permute-start.2 = (f32[9,128,128]{2,1,0:T(8,128)S(1)}, f32[9,128,128]{2,1,0:T(8,128)S(1)}, u32[]{:S(2)}, u32[]{:S(2)}) collective-permute-start(f32[9,128,128]{2,1,0:T(8,128)S(1)} %add.32), channel_id=1, source_target_pairs={{0,4},{1,5},{2,6},{3,7},{4,0},{5,1},{6,2},{7,3},{8,12},{9,13},{10,... | collective-permute-start | bytes 1769480 | tf_op jit(solution)/shard_map/ppermute | solution.py:28
  356.7 13.9 %collective-permute-done.2 = f32[9,128,128]{2,1,0:T(8,128)S(1)} collective-permute-done((f32[9,128,128]{2,1,0:T(8,128)S(1)}, f32[9,128,128]{2,1,0:T(8,128)S(1)}, u32[]{:S(2)}, u32[]{:S(2)}) %collective-permute-start.2) | collective-permute-done | bytes 589856 | tf_op jit(solution)/shard_map/ppermute | solution.py:28
  370.6 0.6 dynamic-slice_add_fusion
  (8 shorter events, 0.1 us)
Async XLA Ops:
  6.5 0.9 copy-start
  6.5 257.8 %all-gather.2.cloned.1.call-start = ((), (), s32[]{:S(2)}) async-start(), calls=%async_computation | async-start | bytes 25559040 | tf_op jit(solution)/shard_map/all_gather | solution.py:20
  8.4 6.9 %copy-start.2 = (s32[9]{0:T(128)S(1)}, s32[9]{0:T(128)}, u32[]{:S(2)}) copy-start(s32[9]{0:T(128)} %param.9) | copy-start | bytes 112
  322.2 49.1 %copy-start.1 = (bf16[3072,32]{0,1:T(8,128)(2,1)S(1)}, bf16[3072,32]{0,1:T(8,128)(2,1)}, u32[]{:S(2)}) copy-start(bf16[3072,32]{0,1:T(8,128)(2,1)} %param.8) | copy-start | bytes 589828
  331.4 3.9 %collective-permute-start = (f32[9,128,128]{2,1,0:T(8,128)S(1)}, f32[9,128,128]{2,1,0:T(8,128)S(1)}, u32[]{:S(2)}, u32[]{:S(2)}) collective-permute-start(f32[9,128,128]{2,1,0:T(8,128)S(1)} %fusion), channel_id=1, source_target_pairs={{0,1},{1,0},{2,3},{3,2},{4,5},{5,4},{6,7},{7,6},{8,9},{9,8},{10,11... | collective-permute-start | bytes 1769480 | tf_op jit(solution)/shard_map/ppermute | solution.py:28
  335.3 17.3 %collective-permute-start.1 = (f32[9,128,128]{2,1,0:T(8,128)S(1)}, f32[9,128,128]{2,1,0:T(8,128)S(1)}, u32[]{:S(2)}, u32[]{:S(2)}) collective-permute-start(f32[9,128,128]{2,1,0:T(8,128)S(1)} %add.31), channel_id=1, source_target_pairs={{0,2},{1,3},{2,0},{3,1},{4,6},{5,7},{6,4},{7,5},{8,10},{9,11},{10,... | collective-permute-start | bytes 1769480 | tf_op jit(solution)/shard_map/ppermute | solution.py:28
  352.7 17.9 %collective-permute-start.2 = (f32[9,128,128]{2,1,0:T(8,128)S(1)}, f32[9,128,128]{2,1,0:T(8,128)S(1)}, u32[]{:S(2)}, u32[]{:S(2)}) collective-permute-start(f32[9,128,128]{2,1,0:T(8,128)S(1)} %add.32), channel_id=1, source_target_pairs={{0,4},{1,5},{2,6},{3,7},{4,0},{5,1},{6,2},{7,3},{8,12},{9,13},{10,... | collective-permute-start | bytes 1769480 | tf_op jit(solution)/shard_map/ppermute | solution.py:28
Sparse Core Ops, SparseCore 0:
  15.4 248.8 all-gather.1
